TPU v7x, 32 devices: a whole 2x2x4 slice. The times are simulated.
32 devices in a mesh: dp: 2 (over x), bytes: 16 (over z, y, core).
Axes of the slice: x: 2, y: 2, z: 4, core: 2. Of those that a mesh axis runs over, the one named last changes fastest.
Arguments:
- byte_queries: bfloat16 [2, 2048, 1024], P('dp', 'bytes'), may hold values from -48 to 48
- byte_keys: bfloat16 [2, 2048, 1024], P('dp', 'bytes'), may hold values from -6 to 6
- byte_values: bfloat16 [2, 2048, 1024], P('dp', 'bytes'), may hold values from -6 to 6
- patch_starts: int32 [2, 16, 12], P('dp', 'bytes'), may hold values from 0 to 128, as said below
- patch_proj: bfloat16 [1024, 4096], P('dp', 'bytes'), may hold values from -0.1875 to 0.1875
- latent_proj: bfloat16 [4096, 4096], P('bytes', 'dp'), may hold values from -0.09375 to 0.09375
- latent_cotangent: bfloat16 [2, 192, 4096], P('dp', 'bytes'), may hold values from -6 to 6
Outputs:
- latent_out: bfloat16 [2, 192, 4096], P('dp', 'bytes')
- pooled_grad: bfloat16 [2, 192, 1024], P('dp', 'bytes')
Inputs may be any that keep to these rules, and one draw needn't show every extreme that they name: `patch_starts`: per shard the first entry is 0, entries increase strictly while below 128 and the rest equal 128; a shard has 6 to 12 patches, and in every stream some shard has exactly 12.
All inputs are finite; a program needn't handle non-finite values.
Results may differ from a plain program's by a relative error of at most 0.025.
Values may be sent and summed in bfloat16 or wider, within the bound.
A program may use at most 64 MiB of HBM per device.

v0:
```python
import math

import jax
import jax.numpy as jnp
from jax import lax
from jax.sharding import PartitionSpec as P

HEAD_L = 64


def shifted(shard, axis, by):
    devices = lax.axis_size(axis)
    pairs = [(i, i + by) for i in range(devices) if 0 <= i + by < devices]
    return lax.ppermute(shard, axis, pairs)


def per_device(
    byte_queries, byte_keys, byte_values, patch_starts, patch_proj, latent_proj, latent_cotangent
):
    rows = byte_queries.shape[1]
    width = byte_queries.shape[2]
    heads = width // HEAD_L
    group_size = math.gcd(heads, 4)
    groups = heads // group_size
    received = {}
    for reach in (2, 1):
        received[reach] = shifted((byte_keys, byte_values), "bytes", reach)
    keys_all = jnp.concatenate([received[2][0][0], received[1][0][0], byte_keys[0]], axis=0)
    values_all = jnp.concatenate([received[2][1][0], received[1][1][0], byte_values[0]], axis=0)
    query_groups = byte_queries[0].reshape(rows, groups, group_size, HEAD_L).transpose(1, 0, 2, 3)
    key_groups = keys_all.reshape(3 * rows, groups, group_size, HEAD_L).transpose(1, 0, 2, 3)
    value_group_list = values_all.reshape(3 * rows, groups, group_size, HEAD_L).transpose(
        1, 0, 2, 3
    )
    qpos = jnp.arange(rows, dtype=jnp.int32)[:, None] + 2 * rows
    kpos = jnp.arange(3 * rows, dtype=jnp.int32)[None, :]
    position = lax.axis_index("bytes")
    reachable = (kpos >= 2 * rows) | (kpos >= rows) & (position >= 1) | (position >= 2)
    allowed = (kpos <= qpos) & (kpos > qpos - 2 * rows) & reachable

    def attend(items):
        query, keys, values = items
        scores = jnp.einsum(
            "ihd,jhd->hij", query, keys, preferred_element_type=jnp.float32
        ) * HEAD_L ** (-0.5)
        scores = jnp.where(allowed[None], scores, -1e30)
        top = jnp.max(scores, axis=-1, keepdims=True)
        expo = jnp.exp(scores - top)
        weights = (expo / jnp.sum(expo, axis=-1, keepdims=True)).astype(jnp.bfloat16)
        mixed = jnp.einsum("hij,jhd->ihd", weights, values, preferred_element_type=jnp.float32)
        return mixed.astype(jnp.bfloat16)

    encoded = lax.map(attend, (query_groups, key_groups, value_group_list))
    encoded = encoded.transpose(1, 0, 2, 3).reshape(rows, width)
    starts = patch_starts[0, 0]
    nexts = jnp.concatenate([starts[1:], jnp.full((1,), rows, jnp.int32)])
    place = jnp.arange(rows, dtype=jnp.int32)[None, :]
    member = (place >= starts[:, None]) & (place < nexts[:, None])
    length = jnp.sum(member.astype(jnp.float32), axis=-1)
    summed = jnp.dot(member.astype(jnp.bfloat16), encoded, preferred_element_type=jnp.float32)
    pooled = (summed / jnp.maximum(length, 1.0)[:, None]).astype(jnp.bfloat16)
    valid = starts < rows
    proj_cols, latent_row_list = (
        lax.all_gather(patch_proj, "dp", axis=0, tiled=True),
        lax.all_gather(latent_proj, "dp", axis=1, tiled=True),
    )
    patches = lax.all_gather(pooled[None], "bytes", axis=1, tiled=True)
    hidden_in = jnp.dot(patches[0], proj_cols, preferred_element_type=jnp.float32)
    activation = jax.nn.silu(hidden_in).astype(jnp.bfloat16)
    piece = activation
    latent = lax.psum_scatter(
        jnp.dot(piece, latent_row_list, preferred_element_type=jnp.float32).astype(jnp.bfloat16),
        "bytes",
        scatter_dimension=0,
        tiled=True,
    )
    cot_all = lax.all_gather(latent_cotangent, "bytes", axis=1, tiled=True)
    back = lax.dot_general(
        cot_all[0], latent_row_list, (((1,), (1,)), ((), ())), preferred_element_type=jnp.float32
    )
    sigma = jax.nn.sigmoid(hidden_in)
    act_grad = (back * sigma * (1.0 + hidden_in * (1.0 - sigma))).astype(jnp.bfloat16)
    piece = act_grad
    grads = lax.psum_scatter(
        lax.dot_general(
            piece, proj_cols, (((1,), (1,)), ((), ())), preferred_element_type=jnp.float32
        ).astype(jnp.bfloat16),
        "bytes",
        scatter_dimension=0,
        tiled=True,
    ).astype(jnp.float32)
    grads = jnp.where(valid[:, None], grads, 0.0)
    return (latent[None], grads.astype(jnp.bfloat16)[None])


def solution(mesh):
    return jax.shard_map(
        per_device,
        mesh=mesh,
        in_specs=(
            P("dp", "bytes", None),
            P("dp", "bytes", None),
            P("dp", "bytes", None),
            P("dp", "bytes", None),
            P("dp", "bytes"),
            P("bytes", "dp"),
            P("dp", "bytes", None),
        ),
        out_specs=(P("dp", "bytes", None), P("dp", "bytes", None)),
        check_vma=False,
    )
```

profile of v0, /device:TPU:0, one launch (start us, length us, event | category | flops | bytes accessed | tf_op | source)
XLA Modules:
  0.0 174.5 jit_solution(3986471334034173944)
XLA Ops:
  7.3 0.7 all-gather.5.cloned.1.call-update
  8.0 4.9 %collective-permute-start = (bf16[1,128,1024]{2,1,0:T(8,128)(2,1)}, bf16[1,128,1024]{2,1,0:T(8,128)(2,1)S(1)}, u32[]{:S(2)}, u32[]{:S(2)}) collective-permute-start(bf16[1,128,1024]{2,1,0:T(8,128)(2,1)} %param.11), channel_id=1, source_target_pairs={{0,2},{1,3},{2,4},{3,5},{4,6},{5,7},{6,8},{7,9},{8,10},{9,11},{10,... | collective-permute-start | bytes 786440 | tf_op jit(solution)/shard_map/ppermute | solution.py:14
  12.9 1.5 collective-permute-start.1
  14.4 3.9 %collective-permute-start.2 = (bf16[1,128,1024]{2,1,0:T(8,128)(2,1)}, bf16[1,128,1024]{2,1,0:T(8,128)(2,1)S(1)}, u32[]{:S(2)}, u32[]{:S(2)}) collective-permute-start(bf16[1,128,1024]{2,1,0:T(8,128)(2,1)} %param.10), channel_id=1, source_target_pairs={{0,2},{1,3},{2,4},{3,5},{4,6},{5,7},{6,8},{7,9},{8,10},{9,11},{10,... | collective-permute-start | bytes 786440 | tf_op jit(solution)/shard_map/ppermute | solution.py:14
  18.2 3.3 %collective-permute-start.3 = (bf16[1,128,1024]{2,1,0:T(8,128)(2,1)}, bf16[1,128,1024]{2,1,0:T(8,128)(2,1)S(1)}, u32[]{:S(2)}, u32[]{:S(2)}) collective-permute-start(bf16[1,128,1024]{2,1,0:T(8,128)(2,1)} %param.10), channel_id=1, source_target_pairs={{0,1},{1,2},{2,3},{3,4},{4,5},{5,6},{6,7},{7,8},{8,9},{9,10},{10,1... | collective-permute-start | bytes 786440 | tf_op jit(solution)/shard_map/ppermute | solution.py:14
  21.5 1.8 %copy.46 = bf16[1,12,4096]{2,0,1:T(2,128)(2,1)} copy(bf16[1,12,4096]{2,1,0:T(8,128)(2,1)} %param.15) | data formatting | bytes 196608 | tf_op args[6]
  23.3 0.7 slice_bitcast_fusion
  24.1 15.4 %all_gather.13 = bf16[1024,256]{1,0:T(8,128)(2,1)S(1)} all-gather(bf16[512,256]{1,0:T(8,128)(2,1)} %param.13), channel_id=1, replica_groups=mesh['dp'=2,'bytes'=16] {'dp'}, dimensions={0}, use_global_device_ids=true | all-gather | bytes 786432 | tf_op jit(solution)/shard_map/all_gather | solution.py:64
  41.0 1.2 maximum_bitcast_fusion
  42.2 11.7 %while.11 = (s32[]{:T(128)}, bf16[4,128,4,64]{1,3,2,0:T(8,128)(2,1)S(1)}, bf16[4,384,4,64]{1,3,2,0:T(8,128)(2,1)}, bf16[4,128,4,64]{1,3,2,0:T(8,128)(2,1)S(1)}, ...) while((s32[]{:T(128)}, ...), condition=%wide.region_3.4_spmd.clone, body=%wide.region_0.3_spmd.clone.sunk | while | flops 77497600 | bytes 3301333 | solution.py:53
  43.1 2.0 %fusion.95 = bf16[4,128,4,64]{1,3,2,0:T(8,128)(2,1)S(1)} fusion(bf16[4,128,4,64]{1,3,2,0:T(8,128)(2,1)S(1)} %get-tuple-element.125, s32[]{:T(128)} %get-tuple-element.124, f32[4,128]{1,0:T(4,128)S(1)} %fusion.93, bf16[4,384,4,64]{1,3,2,0:T(8,128)(2,1)} %get-tuple-element.134, f32[4,128,384]{2,1,0:T(8,128)S(1)} %fusion.94), kind=kOutput, calls=%fused_computation.8.clone.1 | convolution fusion | flops 25789312 | bytes 1838080 | tf_op jit(solution)/shard_map/while/body/eval_jaxpr/hij,jhd->ihd/dot_general | solution.py:50
  46.1 2.0 %fusion.95 = bf16[4,128,4,64]{1,3,2,0:T(8,128)(2,1)S(1)} fusion(bf16[4,128,4,64]{1,3,2,0:T(8,128)(2,1)S(1)} %get-tuple-element.125, s32[]{:T(128)} %get-tuple-element.124, f32[4,128]{1,0:T(4,128)S(1)} %fusion.93, bf16[4,384,4,64]{1,3,2,0:T(8,128)(2,1)} %get-tuple-element.134, f32[4,128,384]{2,1,0:T(8,128)S(1)} %fusion.94), kind=kOutput, calls=%fused_computation.8.clone.1 | convolution fusion | flops 25789312 | bytes 1838080 | tf_op jit(solution)/shard_map/while/body/eval_jaxpr/hij,jhd->ihd/dot_general | solution.py:50
  49.0 2.0 %fusion.95 = bf16[4,128,4,64]{1,3,2,0:T(8,128)(2,1)S(1)} fusion(bf16[4,128,4,64]{1,3,2,0:T(8,128)(2,1)S(1)} %get-tuple-element.125, s32[]{:T(128)} %get-tuple-element.124, f32[4,128]{1,0:T(4,128)S(1)} %fusion.93, bf16[4,384,4,64]{1,3,2,0:T(8,128)(2,1)} %get-tuple-element.134, f32[4,128,384]{2,1,0:T(8,128)S(1)} %fusion.94), kind=kOutput, calls=%fused_computation.8.clone.1 | convolution fusion | flops 25789312 | bytes 1838080 | tf_op jit(solution)/shard_map/while/body/eval_jaxpr/hij,jhd->ihd/dot_general | solution.py:50
  51.9 2.0 %fusion.95 = bf16[4,128,4,64]{1,3,2,0:T(8,128)(2,1)S(1)} fusion(bf16[4,128,4,64]{1,3,2,0:T(8,128)(2,1)S(1)} %get-tuple-element.125, s32[]{:T(128)} %get-tuple-element.124, f32[4,128]{1,0:T(4,128)S(1)} %fusion.93, bf16[4,384,4,64]{1,3,2,0:T(8,128)(2,1)} %get-tuple-element.134, f32[4,128,384]{2,1,0:T(8,128)S(1)} %fusion.94), kind=kOutput, calls=%fused_computation.8.clone.1 | convolution fusion | flops 25789312 | bytes 1838080 | tf_op jit(solution)/shard_map/while/body/eval_jaxpr/hij,jhd->ihd/dot_general | solution.py:50
  54.1 21.0 %all-gather.1 = bf16[16,12,1024]{2,1,0:T(8,128)(2,1)S(1)} all-gather(bf16[1,12,1024]{2,1,0:T(8,128)(2,1)S(1)} %fusion.46), channel_id=2, replica_groups=mesh['dp'=2,'bytes'=16] {'bytes'}, dimensions={0}, use_global_device_ids=true | all-gather | bytes 417792 | tf_op jit(solution)/shard_map/all_gather | solution.py:67
  75.5 2.2 %convolution_convert_fusion.1 = bf16[192,4096]{1,0:T(8,128)(2,1)S(1)} fusion(bf16[256,4096]{1,0:T(8,128)(2,1)} %all-gather.5.cloned.1.call-done, f32[192,256]{1,0:T(8,128)S(1)} %fusion.68), kind=kOutput, calls=%fused_computation.28 | convolution fusion | flops 403685376 | bytes 3866624 | tf_op jit(solution)/shard_map/dot_general | solution.py:72
  77.7 21.2 %all-gather.7.cloned.1.call-done = bf16[1,192,4096]{2,0,1:T(2,128)(2,1)} async-done(((bf16[1,12,4096]{2,0,1:T(2,128)(2,1)}), bf16[1,192,4096]{2,0,1:T(2,128)(2,1)}) %all-gather.7.cloned.1.call-update) | async-done | bytes 1572880 | tf_op jit(solution)/shard_map/all_gather | solution.py:77
  98.9 4.9 %convolution_convert_fusion.2 = bf16[192,1024]{1,0:T(8,128)(2,1)S(1)} fusion(bf16[1024,256]{1,0:T(8,128)(2,1)S(1)} %all_gather.13, bf16[256,4096]{1,0:T(8,128)(2,1)} %all-gather.5.cloned.1.call-done, bf16[1,192,4096]{2,0,1:T(2,128)(2,1)} %all-gather.7.cloned.1.call-done, f32[192,256]{1,0:T(8,128)S(1)} %fusion.68), kind=kOutput, calls=%fused_computation.32 | convolution fusion | flops 503955456 | bytes 4784128 | tf_op jit(solution)/shard_map/dot_general | solution.py:85
  103.8 39.0 %fusion.62 = (bf16[16,4096]{1,0:T(8,128)(2,1)S(1)}, bf16[16,1024]{1,0:T(8,128)(2,1)S(1)}) fusion(bf16[192,4096]{1,0:T(8,128)(2,1)S(1)} %convolution_convert_fusion.1, bf16[192,1024]{1,0:T(8,128)(2,1)S(1)} %convolution_convert_fusion.2), kind=kCustom, calls=%all-reduce-scatter.2 | all-reduce-scatter fusion | flops 1310721 | bytes 2130432
  142.8 1.3 collective-permute-start.10
  144.1 1.3 collective-permute-start.8
  145.4 2.0 %collective-permute-start.9 = (bf16[16,1024]{1,0:T(8,128)(2,1)S(1)}, bf16[16,1024]{1,0:T(8,128)(2,1)S(1)}, u32[]{:S(2)}, u32[]{:S(2)}) collective-permute-start(bf16[16,1024]{1,0:T(8,128)(2,1)S(1)} %get-tuple-element.70), channel_id=1, source_target_pairs={{0,2},{1,3},{2,4},{3,5},{4,6},{5,7},{6,8},{7,9},{8,10},{9,11},{10,... | collective-permute-start | bytes 98312
  147.4 4.2 %collective-permute-start.11 = (bf16[12,1024]{1,0:T(8,128)(2,1)S(1)}, bf16[12,1024]{1,0:T(8,128)(2,1)S(1)}, u32[]{:S(2)}, u32[]{:S(2)}) collective-permute-start(bf16[12,1024]{1,0:T(8,128)(2,1)S(1)} %slice.9), channel_id=1, source_target_pairs={{0,4},{1,5},{2,6},{3,7},{4,8},{5,9},{6,10},{7,11},{8,12},{9,13},{1... | collective-permute-start | bytes 73736
  152.9 1.4 collective-permute-start.4
  154.3 3.4 %collective-permute-start.5 = (bf16[16,4096]{1,0:T(8,128)(2,1)S(1)}, bf16[16,4096]{1,0:T(8,128)(2,1)S(1)}, u32[]{:S(2)}, u32[]{:S(2)}) collective-permute-start(bf16[16,4096]{1,0:T(8,128)(2,1)S(1)} %get-tuple-element.69), channel_id=1, source_target_pairs={{0,2},{1,3},{2,4},{3,5},{4,6},{5,7},{6,8},{7,9},{8,10},{9,11},{10,... | collective-permute-start | bytes 393224
  157.7 3.3 %collective-permute-start.6 = (bf16[16,4096]{1,0:T(8,128)(2,1)S(1)}, bf16[16,4096]{1,0:T(8,128)(2,1)S(1)}, u32[]{:S(2)}, u32[]{:S(2)}) collective-permute-start(bf16[16,4096]{1,0:T(8,128)(2,1)S(1)} %get-tuple-element.69), channel_id=1, source_target_pairs={{0,3},{1,4},{2,5},{3,6},{4,7},{5,8},{6,9},{7,10},{8,11},{9,12},{10... | collective-permute-start | bytes 393224
  161.0 1.9 %collective-permute-start.7 = (bf16[12,4096]{1,0:T(8,128)(2,1)S(1)}, bf16[12,4096]{1,0:T(8,128)(2,1)S(1)}, u32[]{:S(2)}, u32[]{:S(2)}) collective-permute-start(bf16[12,4096]{1,0:T(8,128)(2,1)S(1)} %slice.8), channel_id=1, source_target_pairs={{0,4},{1,5},{2,6},{3,7},{4,8},{5,9},{6,10},{7,11},{8,12},{9,13},{1... | collective-permute-start | bytes 294920
  163.0 0.6 concatenate.33
  163.6 0.7 fusion.52
  164.3 1.4 collective-permute-done.7
  165.7 1.2 concatenate.32
  166.9 0.7 dynamic-slice_bitcast_fusion
  (57 shorter events, 6.5 us)
Async XLA Ops:
  7.2 32.8 %copy-start.1 = (bf16[1,128,1024]{2,1,0:T(8,128)(2,1)S(1)}, bf16[1,128,1024]{2,1,0:T(8,128)(2,1)}, u32[]{:S(2)}) copy-start(bf16[1,128,1024]{2,1,0:T(8,128)(2,1)} %param.11) | copy-start | bytes 786436
  7.2 32.6 %copy-start.2 = (bf16[1,128,1024]{2,1,0:T(8,128)(2,1)S(1)}, bf16[1,128,1024]{2,1,0:T(8,128)(2,1)}, u32[]{:S(2)}) copy-start(bf16[1,128,1024]{2,1,0:T(8,128)(2,1)} %param.10) | copy-start | bytes 786436
  7.2 32.3 %copy-start.4 = (s32[1,1,12]{2,1,0:T(1,128)S(1)}, s32[1,1,12]{2,1,0:T(1,128)}, u32[]{:S(2)}) copy-start(s32[1,1,12]{2,1,0:T(1,128)} %param.12) | copy-start | bytes 148
  7.2 32.9 %copy-start = (bf16[1,128,1024]{2,1,0:T(8,128)(2,1)S(1)}, bf16[1,128,1024]{2,1,0:T(8,128)(2,1)}, u32[]{:S(2)}) copy-start(bf16[1,128,1024]{2,1,0:T(8,128)(2,1)} %param.9) | copy-start | bytes 786436
  7.2 68.3 %all-gather.5.cloned.1.call-start = ((), (), s32[]{:S(2)}) async-start(), calls=%async_computation | async-start | bytes 3145728 | tf_op jit(solution)/shard_map/all_gather | solution.py:65
  7.9 90.9 %all-gather.7.cloned.1.call-start = ((), (), s32[]{:S(2)}) async-start(), calls=%async_computation.1 | async-start | bytes 3342336 | tf_op jit(solution)/shard_map/all_gather | solution.py:77
  8.0 32.3 %collective-permute-start = (bf16[1,128,1024]{2,1,0:T(8,128)(2,1)}, bf16[1,128,1024]{2,1,0:T(8,128)(2,1)S(1)}, u32[]{:S(2)}, u32[]{:S(2)}) collective-permute-start(bf16[1,128,1024]{2,1,0:T(8,128)(2,1)} %param.11), channel_id=1, source_target_pairs={{0,2},{1,3},{2,4},{3,5},{4,6},{5,7},{6,8},{7,9},{8,10},{9,11},{10,... | collective-permute-start | bytes 786440 | tf_op jit(solution)/shard_map/ppermute | solution.py:14
  12.9 27.6 %collective-permute-start.1 = (bf16[1,128,1024]{2,1,0:T(8,128)(2,1)}, bf16[1,128,1024]{2,1,0:T(8,128)(2,1)S(1)}, u32[]{:S(2)}, u32[]{:S(2)}) collective-permute-start(bf16[1,128,1024]{2,1,0:T(8,128)(2,1)} %param.11), channel_id=1, source_target_pairs={{0,1},{1,2},{2,3},{3,4},{4,5},{5,6},{6,7},{7,8},{8,9},{9,10},{10,1... | collective-permute-start | bytes 786440 | tf_op jit(solution)/shard_map/ppermute | solution.py:14
  14.4 26.3 %collective-permute-start.2 = (bf16[1,128,1024]{2,1,0:T(8,128)(2,1)}, bf16[1,128,1024]{2,1,0:T(8,128)(2,1)S(1)}, u32[]{:S(2)}, u32[]{:S(2)}) collective-permute-start(bf16[1,128,1024]{2,1,0:T(8,128)(2,1)} %param.10), channel_id=1, source_target_pairs={{0,2},{1,3},{2,4},{3,5},{4,6},{5,7},{6,8},{7,9},{8,10},{9,11},{10,... | collective-permute-start | bytes 786440 | tf_op jit(solution)/shard_map/ppermute | solution.py:14
  18.2 22.6 %collective-permute-start.3 = (bf16[1,128,1024]{2,1,0:T(8,128)(2,1)}, bf16[1,128,1024]{2,1,0:T(8,128)(2,1)S(1)}, u32[]{:S(2)}, u32[]{:S(2)}) collective-permute-start(bf16[1,128,1024]{2,1,0:T(8,128)(2,1)} %param.10), channel_id=1, source_target_pairs={{0,1},{1,2},{2,3},{3,4},{4,5},{5,6},{6,7},{7,8},{8,9},{9,10},{10,1... | collective-permute-start | bytes 786440 | tf_op jit(solution)/shard_map/ppermute | solution.py:14
  103.8 47.9 %copy-start.3 = (u32[32]{0:T(128)S(1)}, u32[32]{0:T(128)}, u32[]{:S(2)}) copy-start(u32[32]{0:T(128)} %constant.56) | copy-start | bytes 388
  142.8 14.9 %collective-permute-start.10 = (bf16[16,1024]{1,0:T(8,128)(2,1)S(1)}, bf16[16,1024]{1,0:T(8,128)(2,1)S(1)}, u32[]{:S(2)}, u32[]{:S(2)}) collective-permute-start(bf16[16,1024]{1,0:T(8,128)(2,1)S(1)} %get-tuple-element.70), channel_id=1, source_target_pairs={{0,3},{1,4},{2,5},{3,6},{4,7},{5,8},{6,9},{7,10},{8,11},{9,12},{10... | collective-permute-start | bytes 98312
  144.1 16.9 %collective-permute-start.8 = (bf16[16,1024]{1,0:T(8,128)(2,1)S(1)}, bf16[16,1024]{1,0:T(8,128)(2,1)S(1)}, u32[]{:S(2)}, u32[]{:S(2)}) collective-permute-start(bf16[16,1024]{1,0:T(8,128)(2,1)S(1)} %get-tuple-element.70), channel_id=1, source_target_pairs={{0,1},{1,2},{2,3},{3,4},{4,5},{5,6},{6,7},{7,8},{8,9},{9,10},{10,1... | collective-permute-start | bytes 98312
  145.4 17.5 %collective-permute-start.9 = (bf16[16,1024]{1,0:T(8,128)(2,1)S(1)}, bf16[16,1024]{1,0:T(8,128)(2,1)S(1)}, u32[]{:S(2)}, u32[]{:S(2)}) collective-permute-start(bf16[16,1024]{1,0:T(8,128)(2,1)S(1)} %get-tuple-element.70), channel_id=1, source_target_pairs={{0,2},{1,3},{2,4},{3,5},{4,6},{5,7},{6,8},{7,9},{8,10},{9,11},{10,... | collective-permute-start | bytes 98312
  147.4 6.9 %collective-permute-start.11 = (bf16[12,1024]{1,0:T(8,128)(2,1)S(1)}, bf16[12,1024]{1,0:T(8,128)(2,1)S(1)}, u32[]{:S(2)}, u32[]{:S(2)}) collective-permute-start(bf16[12,1024]{1,0:T(8,128)(2,1)S(1)} %slice.9), channel_id=1, source_target_pairs={{0,4},{1,5},{2,6},{3,7},{4,8},{5,9},{6,10},{7,11},{8,12},{9,13},{1... | collective-permute-start | bytes 73736
  152.9 12.8 %collective-permute-start.4 = (bf16[16,4096]{1,0:T(8,128)(2,1)S(1)}, bf16[16,4096]{1,0:T(8,128)(2,1)S(1)}, u32[]{:S(2)}, u32[]{:S(2)}) collective-permute-start(bf16[16,4096]{1,0:T(8,128)(2,1)S(1)} %get-tuple-element.69), channel_id=1, source_target_pairs={{0,1},{1,2},{2,3},{3,4},{4,5},{5,6},{6,7},{7,8},{8,9},{9,10},{10,1... | collective-permute-start | bytes 393224
  154.3 11.4 %collective-permute-start.5 = (bf16[16,4096]{1,0:T(8,128)(2,1)S(1)}, bf16[16,4096]{1,0:T(8,128)(2,1)S(1)}, u32[]{:S(2)}, u32[]{:S(2)}) collective-permute-start(bf16[16,4096]{1,0:T(8,128)(2,1)S(1)} %get-tuple-element.69), channel_id=1, source_target_pairs={{0,2},{1,3},{2,4},{3,5},{4,6},{5,7},{6,8},{7,9},{8,10},{9,11},{10,... | collective-permute-start | bytes 393224
  157.7 8.0 %collective-permute-start.6 = (bf16[16,4096]{1,0:T(8,128)(2,1)S(1)}, bf16[16,4096]{1,0:T(8,128)(2,1)S(1)}, u32[]{:S(2)}, u32[]{:S(2)}) collective-permute-start(bf16[16,4096]{1,0:T(8,128)(2,1)S(1)} %get-tuple-element.69), channel_id=1, source_target_pairs={{0,3},{1,4},{2,5},{3,6},{4,7},{5,8},{6,9},{7,10},{8,11},{9,12},{10... | collective-permute-start | bytes 393224
  161.0 4.7 %collective-permute-start.7 = (bf16[12,4096]{1,0:T(8,128)(2,1)S(1)}, bf16[12,4096]{1,0:T(8,128)(2,1)S(1)}, u32[]{:S(2)}, u32[]{:S(2)}) collective-permute-start(bf16[12,4096]{1,0:T(8,128)(2,1)S(1)} %slice.8), channel_id=1, source_target_pairs={{0,4},{1,5},{2,6},{3,7},{4,8},{5,9},{6,10},{7,11},{8,12},{9,13},{1... | collective-permute-start | bytes 294920
Sparse Core Ops, SparseCore 0:
  9.6 41.4 all-gather.4
  53.4 45.4 all-gather.6
where the time goes:
time: 176 us; the launch traced here: 174 us
  blocking collectives  75.4 us (43%)
  starting transfers between devices  32.3 us (18%)
  waiting for transfers between devices  23.4 us (13%)
  matrix products  18.7 us (11%)
  between operations  15.1 us (9%)
  local copies, waits for them, and re-layouts  6.94 us (4%)
  other arithmetic  2.54 us (1%)
    unnamed x1, blocking collectives  39 us
    all_gather x1, waiting for transfers between devices, per_device(): cot_all = lax.all_gather(latent_cotangent, 'bytes', axis=1, tiled=True)  21.2 us
    all_gather x1, blocking collectives, per_device(): patches = lax.all_gather(pooled[None], 'bytes', axis=1, tiled=True)  21 us
    unnamed x8, starting transfers between devices  18.7 us
    all_gather x1, blocking collectives, per_device(): lax.all_gather(patch_proj, 'dp', axis=0, tiled=True)  15.4 us
    ppermute x4, starting transfers between devices, shifted(): return lax.ppermute(shard, axis, pairs)  13.5 us
    dot_general x4, matrix products, attend(): jnp.einsum('hij,jhd->ihd', weights, values, preferred_element_type=jnp.fl...  7.92 us
    dot_general x1, matrix products, per_device(): lax.dot_general(piece, proj_cols, (((1,), (1,)), ((), ())), preferred_ele...  4.87 us
  transfers between devices with their start and end apart: 14, of which 2 were waited for; matrix products, arithmetic and copies ran while one was open for 12% of the time, Pallas kernels for 0%

commit v1 on v0

v1 whole, which is shorter than its diff:
```python
import functools

import jax
import jax.numpy as jnp
from jax import lax
from jax.experimental import pallas as pl
from jax.experimental.pallas import tpu as pltpu
from jax.sharding import PartitionSpec as P

HEAD_L = 64
MESH = pl.DeviceIdType.MESH
SLAB = 16
F32 = jnp.float32
BF16 = jnp.bfloat16
NT = (((1,), (1,)), ((), ()))


def remote(src, dst, send, recv, target):
    return pltpu.make_async_remote_copy(
        src_ref=src, dst_ref=dst, send_sem=send, recv_sem=recv, device_id=target, device_id_type=MESH
    )


def kernel(
    n,
    exchange,
    starts_ref,
    q_ref,
    k_ref,
    v_ref,
    cot_ref,
    pp_ref,
    lp_ref,
    latent_ref,
    grad_ref,
    kbuf,
    vbuf,
    enc,
    pool,
    cots,
    pp,
    lp,
    act,
    own,
    sib_out,
    sib_in,
    y_out,
    y_in,
    z_out,
    z_in,
    loc_sem,
    wsend,
    wrecv,
    ksend,
    krecv,
    ssend,
    srecv,
    pzs,
    pzr,
    pfs,
    pfr,
    czs,
    czr,
    cfs,
    cfr,
    rss,
    rsr,
    rys,
    ryr,
    rzs,
    rzr,
):
    rows, width = q_ref.shape
    d = lax.axis_index("dp")
    b = lax.axis_index("bytes")
    nz = n // 4
    chips = n // 2
    chip = b // 2
    core = b % 2
    y = chip % 2
    z = chip // 2
    groups = kbuf.shape[2] // 256
    chunks = own.shape[0]
    lat_chunks = chunks - 1
    cw = own.shape[2]
    slots = latent_ref.shape[0]
    half = n // 2 * SLAB
    quarter = half // 2

    sibling = {"bytes": chip * 2 + 1 - core}
    y_peer = {"bytes": (z * 2 + 1 - y) * 2 + core}
    onward = {"bytes": lax.rem(chip + 1, chips) * 2 + core}
    other = jnp.where(y == 1, lax.rem(chip + 1, chips), lax.rem(chip + chips - 1, chips))

    def z_peer(j):
        return {"bytes": (lax.rem(z + j, nz) * 2 + y) * 2 + core}

    def slab(zz):
        return pl.ds(pl.multiple_of(((core * 2 + y) * nz + zz) * SLAB, SLAB), SLAB)

    y_half = pl.ds(pl.multiple_of((core * 2 + y) * quarter, SLAB), quarter)
    y_half_in = pl.ds(pl.multiple_of((core * 2 + 1 - y) * quarter, SLAB), quarter)
    c_half = pl.ds(pl.multiple_of(core * half, SLAB), half)
    c_half_in = pl.ds(pl.multiple_of((1 - core) * half, SLAB), half)

    if exchange:
        p_rows, l_cols = pp_ref.shape[0], lp_ref.shape[1]
        p_own = pl.ds(pl.multiple_of(d * p_rows, 256), p_rows)
        p_got = pl.ds(pl.multiple_of((1 - d) * p_rows, 256), p_rows)
        l_own = pl.ds(pl.multiple_of(d * l_cols, 256), l_cols)
        l_got = pl.ds(pl.multiple_of((1 - d) * l_cols, 256), l_cols)
        partner = {"dp": 1 - d}
        p_local = pltpu.make_async_copy(pp_ref, pp.at[p_own], loc_sem.at[0])
        l_local = pltpu.make_async_copy(lp_ref, lp.at[:, l_own], loc_sem.at[1])
    else:
        p_local = pltpu.make_async_copy(pp_ref, pp, loc_sem.at[0])
        l_local = pltpu.make_async_copy(lp_ref, lp, loc_sem.at[1])

    barrier = pltpu.get_barrier_semaphore()
    greeted = [sibling, y_peer, {"bytes": other * 2 + core}] + [z_peer(j) for j in range(1, nz)]
    if exchange:
        greeted.append(partner)
    for device in greeted:
        pl.semaphore_signal(barrier, inc=1, device_id=device, device_id_type=MESH)
    p_local.start()
    l_local.start()
    my_slab = slab(z)
    cots[my_slab, :] = jnp.zeros((SLAB, cots.shape[1]), BF16)
    cots[pl.ds(pl.multiple_of(((core * 2 + y) * nz + z) * SLAB, SLAB), slots), :] = cot_ref[...]
    pl.semaphore_wait(barrier, len(greeted))

    def cols(g):
        return pl.ds(pl.multiple_of(g * 256, 256), 256)

    def ahead(t, g):
        ref, buf = ((k_ref, kbuf), (v_ref, vbuf))[t]
        return remote(ref.at[:, cols(g)], buf.at[0, :, cols(g)], ksend.at[t, g], krecv.at[t, g], onward)

    def across(t, g):
        ref, buf = ((k_ref, kbuf), (v_ref, vbuf))[t]
        return remote(ref.at[:, cols(g)], buf.at[1, :, cols(g)], ssend.at[t, g], srecv.at[t, g], sibling)

    def passed(t, g):
        buf = (kbuf, vbuf)[t]
        return remote(buf.at[0, :, cols(g)], buf.at[1, :, cols(g)], ssend.at[t, g], srecv.at[t, g], sibling)

    @pl.when(chip < chips - 1)
    def _():
        @pl.loop(0, groups)
        def _(g):
            ahead(0, g).start()
            ahead(1, g).start()

    @pl.when(core == 0)
    def _():
        @pl.loop(0, groups)
        def _(g):
            across(0, g).start()
            across(1, g).start()

    if exchange:
        p_remote = remote(pp_ref, pp.at[p_own], wsend.at[0], wrecv.at[0], partner)
        l_remote = remote(lp_ref, lp.at[:, l_own], wsend.at[1], wrecv.at[1], partner)
        p_remote.start()
        l_remote.start()
    cot_z = [
        remote(cots.at[my_slab], cots.at[my_slab], czs.at[j - 1], czr.at[j - 1], z_peer(j))
        for j in range(1, nz)
    ]
    for copy in cot_z:
        copy.start()

    @pl.when(chip == 0)
    def _():
        kbuf[0] = jnp.zeros((rows, width), BF16)
        vbuf[0] = jnp.zeros((rows, width), BF16)

    @pl.when(b == 0)
    def _():
        kbuf[1] = jnp.zeros((rows, width), BF16)
        vbuf[1] = jnp.zeros((rows, width), BF16)

    slot_row = lax.broadcasted_iota(jnp.int32, (SLAB, rows), 0)
    place = lax.broadcasted_iota(jnp.int32, (SLAB, rows), 1)
    first = jnp.full((SLAB, rows), rows, jnp.int32)
    last = jnp.full((SLAB, rows), rows, jnp.int32)
    for p in range(slots):
        first = jnp.where(slot_row == p, starts_ref[0, p], first)
        if p + 1 < slots:
            last = jnp.where(slot_row == p, starts_ref[0, p + 1], last)
    member = jnp.where((place >= first) & (place < last), 1.0, 0.0).astype(F32)
    length = jnp.maximum(jnp.sum(member, axis=1, keepdims=True), 1.0)
    member = member.astype(BF16)
    valid = jnp.max(first, axis=1, keepdims=True) < rows

    lane = lax.broadcasted_iota(jnp.int32, (rows, 128), 1)
    query_row = lax.broadcasted_iota(jnp.int32, (2 * rows, rows), 0)
    query_row = jnp.where(query_row >= rows, query_row - rows, query_row)
    causal = lax.broadcasted_iota(jnp.int32, (2 * rows, rows), 1) <= query_row
    low = lane < HEAD_L
    far_bias = jnp.where(chip >= 1, 0.0, -1e30).astype(F32)
    mid_bias = jnp.where(b >= 1, 0.0, -1e30).astype(F32)

    def await_group(t, g):
        @pl.when(chip >= 1)
        def _():
            ahead(t, g).wait_recv()

        @pl.when((core == 1) & (chip >= 1))
        def _():
            passed(t, g).start()

        @pl.when((core == 1) | (chip >= 1))
        def _():
            across(t, g).wait_recv()

    @pl.loop(0, groups)
    def _(g):
        await_group(0, g)
        await_group(1, g)

        for pair in range(2):
            at = pl.ds(pl.multiple_of(g * 256 + pair * 128, 128), 128)
            q = q_ref[:, at].astype(F32) * HEAD_L ** (-0.5)
            q2 = jnp.concatenate([jnp.where(low, q, 0.0), jnp.where(low, 0.0, q)], axis=0).astype(BF16)
            s_own = lax.dot_general(q2, k_ref[:, at], NT, preferred_element_type=F32)
            s_mid = lax.dot_general(q2, kbuf[1, :, at], NT, preferred_element_type=F32) + mid_bias
            s_far = lax.dot_general(q2, kbuf[0, :, at], NT, preferred_element_type=F32) + far_bias
            s_two = jnp.where(causal, s_own, s_far)
            top = jnp.max(jnp.maximum(s_two, s_mid), axis=1, keepdims=True)
            e_two = jnp.exp(s_two - top)
            e_mid = jnp.exp(s_mid - top)
            total = jnp.sum(e_two + e_mid, axis=1, keepdims=True)
            e_own = jnp.where(causal, e_two, 0.0).astype(BF16)
            e_far = jnp.where(causal, 0.0, e_two).astype(BF16)
            mixed = jnp.dot(e_own, v_ref[:, at], preferred_element_type=F32)
            mixed += jnp.dot(e_mid.astype(BF16), vbuf[1, :, at], preferred_element_type=F32)
            mixed += jnp.dot(e_far, vbuf[0, :, at], preferred_element_type=F32)
            mixed = mixed / total
            enc[:, at] = jnp.where(low, mixed[:rows], mixed[rows:]).astype(BF16)
        summed = jnp.dot(member, enc[:, cols(g)], preferred_element_type=F32)
        pool[my_slab, cols(g)] = (summed / length).astype(BF16)

    pool_z = [
        remote(pool.at[my_slab], pool.at[my_slab], pzs.at[j - 1], pzr.at[j - 1], z_peer(j))
        for j in range(1, nz)
    ]
    for copy in pool_z:
        copy.start()
    cot_y = remote(cots.at[y_half], cots.at[y_half], cfs.at[0], cfr.at[0], y_peer)
    cot_c = remote(cots.at[c_half], cots.at[c_half], cfs.at[1], cfr.at[1], sibling)
    pool_y = remote(pool.at[y_half], pool.at[y_half], pfs.at[0], pfr.at[0], y_peer)
    pool_c = remote(pool.at[c_half], pool.at[c_half], pfs.at[1], pfr.at[1], sibling)

    def await_z(buf, sends, recvs):
        for j in range(1, nz):
            from_slab = slab(lax.rem(z + nz - j, nz))
            remote(buf.at[from_slab], buf.at[from_slab], sends.at[j - 1], recvs.at[j - 1], z_peer(j)).wait_recv()

    await_z(pool, pzs, pzr)
    pool_y.start()
    await_z(cots, czs, czr)
    cot_y.start()
    remote(pool.at[y_half_in], pool.at[y_half_in], pfs.at[0], pfr.at[0], y_peer).wait_recv()
    pool_c.start()
    remote(pool.at[c_half_in], pool.at[c_half_in], pfs.at[1], pfr.at[1], sibling).wait_recv()

    p_local.wait()
    if exchange:
        remote(pp_ref, pp.at[p_got], wsend.at[0], wrecv.at[0], partner).wait_recv()
    hidden = jnp.dot(pool[...], pp[...], preferred_element_type=F32)
    sigma = 1.0 / (1.0 + jnp.exp(-hidden))
    act[...] = (hidden * sigma).astype(BF16)
    slope = sigma * (1.0 + hidden * (1.0 - sigma))

    l_local.wait()
    if exchange:
        remote(lp_ref, lp.at[:, l_got], wsend.at[1], wrecv.at[1], partner).wait_recv()

    mine = pl.ds(pl.multiple_of(core * half, SLAB), half)
    theirs = pl.ds(pl.multiple_of((1 - core) * half, SLAB), half)

    def to_sibling(c):
        return remote(sib_out.at[c], sib_in.at[c], rss.at[c], rsr.at[c], sibling)

    def to_y(c):
        return remote(y_out.at[c], y_in.at[c], rys.at[c], ryr.at[c], y_peer)

    def to_z(c, j):
        return remote(z_out.at[c, j - 1], z_in.at[c, j - 1], rzs.at[c, j - 1], rzr.at[c, j - 1], z_peer(j))

    def c_cols(c):
        return pl.ds(pl.multiple_of(c * cw, 128), cw)

    @pl.loop(0, lat_chunks)
    def _(c):
        w = lp[:, c_cols(c)]
        sib_out[c] = jnp.dot(act[theirs, :], w, preferred_element_type=F32).astype(BF16)
        to_sibling(c).start()
        own[c] = jnp.dot(act[mine, :], w, preferred_element_type=F32)

    remote(cots.at[y_half_in], cots.at[y_half_in], cfs.at[0], cfr.at[0], y_peer).wait_recv()
    cot_c.start()

    def y_step(c):
        to_sibling(c).wait_recv()
        there = pl.ds(pl.multiple_of((1 - y) * quarter, SLAB), quarter)
        here = pl.ds(pl.multiple_of(y * quarter, SLAB), quarter)
        y_out[c] = (own[c, there, :] + sib_in[c, there, :].astype(F32)).astype(BF16)
        to_y(c).start()
        own[c, here, :] = own[c, here, :] + sib_in[c, here, :].astype(F32)

    def z_step(c):
        to_y(c).wait_recv()
        for j in range(1, nz):
            zz = lax.rem(z + j, nz)
            at = pl.ds(pl.multiple_of(y * quarter + zz * SLAB, SLAB), SLAB)
            got = pl.ds(pl.multiple_of(zz * SLAB, SLAB), SLAB)
            z_out[c, j - 1] = (own[c, at, :] + y_in[c, got, :].astype(F32)).astype(BF16)
            to_z(c, j).start()

    def last_step(c):
        at = pl.ds(pl.multiple_of(y * quarter + z * SLAB, SLAB), SLAB)
        got = pl.ds(pl.multiple_of(z * SLAB, SLAB), SLAB)
        total = own[c, at, :] + y_in[c, got, :].astype(F32)
        for j in range(1, nz):
            to_z(c, j).wait_recv()
            total = total + z_in[c, j - 1].astype(F32)
        return total

    pl.loop(0, lat_chunks)(y_step)

    remote(cots.at[c_half_in], cots.at[c_half_in], cfs.at[1], cfr.at[1], sibling).wait_recv()
    back = lax.dot_general(cots[...], lp[...], NT, preferred_element_type=F32)
    act[...] = (back * slope).astype(BF16)
    g = lat_chunks
    sib_out[g] = lax.dot_general(act[theirs, :], pp[...], NT, preferred_element_type=F32).astype(BF16)
    to_sibling(g).start()
    own[g] = lax.dot_general(act[mine, :], pp[...], NT, preferred_element_type=F32)
    y_step(g)

    pl.loop(0, chunks)(z_step)

    @pl.loop(0, lat_chunks)
    def _(c):
        latent_ref[:, c_cols(c)] = last_step(c)[:slots].astype(BF16)

    grad_ref[...] = jnp.where(valid, last_step(g), 0.0)[:slots].astype(BF16)

    @pl.when(chip < chips - 1)
    def _():
        @pl.loop(0, groups)
        def _(g):
            ahead(0, g).wait_send()
            ahead(1, g).wait_send()

    @pl.when((core == 0) | (chip >= 1))
    def _():
        @pl.loop(0, groups)
        def _(g):
            across(0, g).wait_send()
            across(1, g).wait_send()

    if exchange:
        p_remote.wait_send()
        l_remote.wait_send()
    for copy in cot_z + pool_z + [cot_y, cot_c, pool_y, pool_c]:
        copy.wait_send()

    @pl.loop(0, chunks)
    def _(c):
        to_sibling(c).wait_send()
        to_y(c).wait_send()
        for j in range(1, nz):
            to_z(c, j).wait_send()


def per_device(
    n,
    exchange,
    byte_queries,
    byte_keys,
    byte_values,
    patch_starts,
    patch_proj,
    latent_proj,
    latent_cotangent,
):
    rows, width = byte_queries.shape[1:]
    slots, wide = latent_cotangent.shape[1:]
    if not exchange:
        patch_proj = lax.all_gather(patch_proj, "dp", axis=0, tiled=True)
        latent_proj = lax.all_gather(latent_proj, "dp", axis=1, tiled=True)
    block = patch_proj.shape[1]
    nz = n // 4
    cw = width
    chunks = wide // cw + 1
    groups = width // 256
    half = n // 2 * SLAB
    vmem = pl.BlockSpec(memory_space=pltpu.VMEM)
    hbm = pl.BlockSpec(memory_space=pl.ANY)
    dma = pltpu.SemaphoreType.DMA
    latent, grads = pl.pallas_call(
        functools.partial(kernel, n, exchange),
        out_shape=(
            jax.ShapeDtypeStruct((slots, wide), BF16),
            jax.ShapeDtypeStruct((slots, width), BF16),
        ),
        in_specs=[pl.BlockSpec(memory_space=pltpu.SMEM), vmem, vmem, vmem, vmem, hbm, hbm],
        out_specs=(vmem, vmem),
        scratch_shapes=[
            pltpu.VMEM((2, rows, width), BF16),
            pltpu.VMEM((2, rows, width), BF16),
            pltpu.VMEM((rows, width), BF16),
            pltpu.VMEM((n * SLAB, width), BF16),
            pltpu.VMEM((n * SLAB, wide), BF16),
            pltpu.VMEM((width, block), BF16),
            pltpu.VMEM((block, wide), BF16),
            pltpu.VMEM((n * SLAB, block), BF16),
            pltpu.VMEM((chunks, half, cw), F32),
            pltpu.VMEM((chunks, half, cw), BF16),
            pltpu.VMEM((chunks, half, cw), BF16),
            pltpu.VMEM((chunks, half // 2, cw), BF16),
            pltpu.VMEM((chunks, half // 2, cw), BF16),
            pltpu.VMEM((chunks, nz - 1, SLAB, cw), BF16),
            pltpu.VMEM((chunks, nz - 1, SLAB, cw), BF16),
            dma((2,)),
            dma((2,)),
            dma((2,)),
            dma((2, groups)),
            dma((2, groups)),
            dma((2, groups)),
            dma((2, groups)),
            dma((nz - 1,)),
            dma((nz - 1,)),
            dma((2,)),
            dma((2,)),
            dma((nz - 1,)),
            dma((nz - 1,)),
            dma((2,)),
            dma((2,)),
            dma((chunks,)),
            dma((chunks,)),
            dma((chunks,)),
            dma((chunks,)),
            dma((chunks, nz - 1)),
            dma((chunks, nz - 1)),
        ],
        compiler_params=pltpu.CompilerParams(
            collective_id=0, has_side_effects=True, vmem_limit_bytes=44 * 2**20
        ),
        cost_estimate=pl.CostEstimate(flops=2 * 10**9, bytes_accessed=4 * 10**6, transcendentals=10**6),
    )(
        patch_starts[0],
        byte_queries[0],
        byte_keys[0],
        byte_values[0],
        latent_cotangent[0],
        patch_proj,
        latent_proj,
    )
    return latent[None], grads[None]


def solution(mesh):
    n = mesh.shape["bytes"]
    return jax.shard_map(
        functools.partial(per_device, n, mesh.shape["dp"] == 2),
        mesh=mesh,
        in_specs=(
            P("dp", "bytes", None),
            P("dp", "bytes", None),
            P("dp", "bytes", None),
            P("dp", "bytes", None),
            P("dp", "bytes"),
            P("bytes", "dp"),
            P("dp", "bytes", None),
        ),
        out_specs=(P("dp", "bytes", None), P("dp", "bytes", None)),
        check_vma=False,
    )
```

time: 176 us -> 79.1 us (0.45)
  blocking collectives: 75.4 us -> 0 us
  Pallas kernels: 0 us -> 70.3 us
  starting transfers between devices: 32.3 us -> 0 us
  waiting for transfers between devices: 23.4 us -> 0 us
  matrix products: 18.7 us -> 0 us
  between operations: 15.1 us -> 0.66 us
  other arithmetic: 2.54 us -> 0 us
    pallas_call x0 -> x1, Pallas kernels: none -> 70.3 us  [per_device(): pl.pallas_call(functools.partial(kernel, n, exchange), out_shape=(jax.Sha...]
    unnamed x1 -> x0, blocking collectives: 39 us -> none
    all_gather x2 -> x0, blocking collectives: 36.4 us -> none  [the longest x1 21 us: per_device(): patches = lax.all_gather(pooled[None], 'bytes', axis=1, tiled=True)]
    all_gather x2 -> x0, waiting for transfers between devices: 21.2 us -> none  [the longest x1 21.2 us: per_device(): cot_all = lax.all_gather(latent_cotangent, 'bytes', axis=1, tiled=True)]
    unnamed x8 -> x0, starting transfers between devices: 18.7 us -> none
    dot_general x12 -> x0, matrix products: 16.7 us -> none  [the longest x4 7.92 us: attend(): jnp.einsum('hij,jhd->ihd', weights, values, preferred_element_type=jnp.fl...]
    ppermute x4 -> x0, starting transfers between devices: 13.5 us -> none  [shifted(): return lax.ppermute(shard, axis, pairs)]
    unnamed x20 -> x16, local copies, waits for them, and re-layouts: 4.84 us -> 7.85 us
  transfers between devices with their start and end apart: 14 -> 0, of which waited for: 2 -> 0; matrix products, arithmetic and copies ran while one was open for 12% -> 0% of each run, Pallas kernels for 0% -> 0%
where the time goes in v1:
time: 79.1 us; the launch traced here: 78.8 us
  Pallas kernels  70.3 us (89%)
  local copies, waits for them, and re-layouts  7.85 us (10%)
    pallas_call x1, Pallas kernels, per_device(): pl.pallas_call(functools.partial(kernel, n, exchange), out_shape=(jax.Sha...  70.3 us
    unnamed x16, local copies, waits for them, and re-layouts  7.85 us

profile of v1, /device:TPU:0, one launch (start us, length us, event | category | flops | bytes accessed | tf_op | source)
XLA Modules:
  0.0 78.8 jit_solution(7064292053826586370)
XLA Ops:
  0.6 0.0 copy-start.6
  0.6 0.6 copy-done.6
  1.3 0.0 copy-start
  1.3 1.2 %copy-done = bf16[256,2048]{1,0:T(8,128)(2,1)S(1)} copy-done((bf16[256,2048]{1,0:T(8,128)(2,1)S(1)}, bf16[256,2048]{1,0:T(8,128)(2,1)}, u32[]{:S(2)}) %copy-start) | copy-done | bytes 1048600
  2.5 0.0 copy-start.1
  2.5 0.9 %copy-done.1 = bf16[1,128,1024]{2,1,0:T(8,128)(2,1)S(1)} copy-done((bf16[1,128,1024]{2,1,0:T(8,128)(2,1)S(1)}, bf16[1,128,1024]{2,1,0:T(8,128)(2,1)}, u32[]{:S(2)}) %copy-start.1) | copy-done | bytes 262168
  3.5 0.0 copy-start.2
  3.5 0.9 %copy-done.2 = bf16[1,128,1024]{2,1,0:T(8,128)(2,1)S(1)} copy-done((bf16[1,128,1024]{2,1,0:T(8,128)(2,1)S(1)}, bf16[1,128,1024]{2,1,0:T(8,128)(2,1)}, u32[]{:S(2)}) %copy-start.2) | copy-done | bytes 262168
  4.4 0.0 copy-start.3
  4.4 0.9 %copy-done.3 = bf16[1,128,1024]{2,1,0:T(8,128)(2,1)S(1)} copy-done((bf16[1,128,1024]{2,1,0:T(8,128)(2,1)S(1)}, bf16[1,128,1024]{2,1,0:T(8,128)(2,1)}, u32[]{:S(2)}) %copy-start.3) | copy-done | bytes 262168
  5.4 0.0 copy-start.4
  5.4 0.9 %copy-done.4 = bf16[512,256]{1,0:T(8,128)(2,1)S(1)} copy-done((bf16[512,256]{1,0:T(8,128)(2,1)S(1)}, bf16[512,256]{1,0:T(8,128)(2,1)}, u32[]{:S(2)}) %copy-start.4) | copy-done | bytes 262168
  6.3 0.0 copy-start.5
  6.3 0.9 %copy-done.5 = bf16[1,12,4096]{2,1,0:T(8,128)(2,1)S(1)} copy-done((bf16[1,12,4096]{2,1,0:T(8,128)(2,1)S(1)}, bf16[1,12,4096]{2,1,0:T(8,128)(2,1)}, u32[]{:S(2)}) %copy-start.5) | copy-done | bytes 98328
  7.2 70.3 %shard_map.86 = (bf16[12,4096]{1,0:T(8,128)(2,1)S(1)}, bf16[12,1024]{1,0:T(8,128)(2,1)S(1)}) custom-call(s32[1,12]{1,0:T(1,128)S(1)} %bitcast.13, bf16[128,1024]{1,0:T(8,128)(2,1)S(1)} %bitcast.9, bf16[128,1024]{1,0:T(8,128)(2,1)S(1)} %bitcast.10, bf16[128,1024]{1,0:T(8,128)(2,1)S(1)} %bitcast.11, bf16[12,4096]{1,0:T(8,128)(2,1)S(1)} %bitcast.12, ...), custom_call_target="tpu_custom_call" | custom-call | flops 2000000000 | bytes 4000000 | tf_op jit(solution)/shard_map/pallas_call | solution.py:403
  77.5 0.7 copy.11
  78.2 0.6 copy.12
Async XLA Ops:
  0.6 0.7 copy-start.6
  1.3 1.2 %copy-start = (bf16[256,2048]{1,0:T(8,128)(2,1)S(1)}, bf16[256,2048]{1,0:T(8,128)(2,1)}, u32[]{:S(2)}) copy-start(bf16[256,2048]{1,0:T(8,128)(2,1)} %lp_ref.1) | copy-start | bytes 3145732
  2.5 0.9 %copy-start.1 = (bf16[1,128,1024]{2,1,0:T(8,128)(2,1)S(1)}, bf16[1,128,1024]{2,1,0:T(8,128)(2,1)}, u32[]{:S(2)}) copy-start(bf16[1,128,1024]{2,1,0:T(8,128)(2,1)} %param.7) | copy-start | bytes 786436
  3.5 0.9 %copy-start.2 = (bf16[1,128,1024]{2,1,0:T(8,128)(2,1)S(1)}, bf16[1,128,1024]{2,1,0:T(8,128)(2,1)}, u32[]{:S(2)}) copy-start(bf16[1,128,1024]{2,1,0:T(8,128)(2,1)} %param.8) | copy-start | bytes 786436
  4.4 0.9 %copy-start.3 = (bf16[1,128,1024]{2,1,0:T(8,128)(2,1)S(1)}, bf16[1,128,1024]{2,1,0:T(8,128)(2,1)}, u32[]{:S(2)}) copy-start(bf16[1,128,1024]{2,1,0:T(8,128)(2,1)} %param.9) | copy-start | bytes 786436
  5.4 0.9 %copy-start.4 = (bf16[512,256]{1,0:T(8,128)(2,1)S(1)}, bf16[512,256]{1,0:T(8,128)(2,1)}, u32[]{:S(2)}) copy-start(bf16[512,256]{1,0:T(8,128)(2,1)} %pp_ref.1) | copy-start | bytes 786436
  6.3 0.9 %copy-start.5 = (bf16[1,12,4096]{2,1,0:T(8,128)(2,1)S(1)}, bf16[1,12,4096]{2,1,0:T(8,128)(2,1)}, u32[]{:S(2)}) copy-start(bf16[1,12,4096]{2,1,0:T(8,128)(2,1)} %param.13) | copy-start | bytes 294916

commit v2 on v1

--- a/solution.py
+++ b/solution.py
@@ -24,15 +24,20 @@
 def kernel(
     n,
     exchange,
+    starts_hbm,
+    q_hbm,
+    k_hbm,
+    v_hbm,
+    cot_hbm,
+    pp_ref,
+    lp_ref,
+    latent_ref,
+    grad_ref,
     starts_ref,
     q_ref,
     k_ref,
     v_ref,
     cot_ref,
-    pp_ref,
-    lp_ref,
-    latent_ref,
-    grad_ref,
     kbuf,
     vbuf,
     enc,
@@ -48,6 +53,7 @@
     y_in,
     z_out,
     z_in,
+    in_sem,
     loc_sem,
     wsend,
     wrecv,
@@ -86,6 +92,7 @@
     slots = latent_ref.shape[0]
     half = n // 2 * SLAB
     quarter = half // 2
+    tight = n // 2 * slots
 
     sibling = {"bytes": chip * 2 + 1 - core}
     y_peer = {"bytes": (z * 2 + 1 - y) * 2 + core}
@@ -116,16 +123,29 @@
         p_local = pltpu.make_async_copy(pp_ref, pp, loc_sem.at[0])
         l_local = pltpu.make_async_copy(lp_ref, lp, loc_sem.at[1])
 
+    loads = [
+        pltpu.make_async_copy(src, dst, in_sem.at[i])
+        for i, (src, dst) in enumerate(
+            (
+                (cot_hbm, cot_ref),
+                (starts_hbm, starts_ref),
+                (q_hbm, q_ref),
+                (k_hbm, k_ref),
+                (v_hbm, v_ref),
+            )
+        )
+    ]
     barrier = pltpu.get_barrier_semaphore()
     greeted = [sibling, y_peer, {"bytes": other * 2 + core}] + [z_peer(j) for j in range(1, nz)]
     if exchange:
         greeted.append(partner)
     for device in greeted:
         pl.semaphore_signal(barrier, inc=1, device_id=device, device_id_type=MESH)
-    p_local.start()
-    l_local.start()
+    for copy in loads:
+        copy.start()
     my_slab = slab(z)
     cots[my_slab, :] = jnp.zeros((SLAB, cots.shape[1]), BF16)
+    loads[0].wait()
     cots[pl.ds(pl.multiple_of(((core * 2 + y) * nz + z) * SLAB, SLAB), slots), :] = cot_ref[...]
     pl.semaphore_wait(barrier, len(greeted))
 
@@ -133,11 +153,11 @@
         return pl.ds(pl.multiple_of(g * 256, 256), 256)
 
     def ahead(t, g):
-        ref, buf = ((k_ref, kbuf), (v_ref, vbuf))[t]
+        ref, buf = ((k_hbm, kbuf), (v_hbm, vbuf))[t]
         return remote(ref.at[:, cols(g)], buf.at[0, :, cols(g)], ksend.at[t, g], krecv.at[t, g], onward)
 
     def across(t, g):
-        ref, buf = ((k_ref, kbuf), (v_ref, vbuf))[t]
+        ref, buf = ((k_hbm, kbuf), (v_hbm, vbuf))[t]
         return remote(ref.at[:, cols(g)], buf.at[1, :, cols(g)], ssend.at[t, g], srecv.at[t, g], sibling)
 
     def passed(t, g):
@@ -169,6 +189,8 @@
     ]
     for copy in cot_z:
         copy.start()
+    p_local.start()
+    l_local.start()
 
     @pl.when(chip == 0)
     def _():
@@ -180,6 +202,7 @@
         kbuf[1] = jnp.zeros((rows, width), BF16)
         vbuf[1] = jnp.zeros((rows, width), BF16)
 
+    loads[1].wait()
     slot_row = lax.broadcasted_iota(jnp.int32, (SLAB, rows), 0)
     place = lax.broadcasted_iota(jnp.int32, (SLAB, rows), 1)
     first = jnp.full((SLAB, rows), rows, jnp.int32)
@@ -214,10 +237,26 @@
         def _():
             across(t, g).wait_recv()
 
+    cot_y = remote(cots.at[y_half], cots.at[y_half], cfs.at[0], cfr.at[0], y_peer)
+    cot_c = remote(cots.at[c_half], cots.at[c_half], cfs.at[1], cfr.at[1], sibling)
+
+    def await_z(buf, sends, recvs):
+        for j in range(1, nz):
+            from_slab = slab(lax.rem(z + nz - j, nz))
+            remote(buf.at[from_slab], buf.at[from_slab], sends.at[j - 1], recvs.at[j - 1], z_peer(j)).wait_recv()
+
+    for copy in loads[2:]:
+        copy.wait()
+
     @pl.loop(0, groups)
     def _(g):
         await_group(0, g)
         await_group(1, g)
+
+        @pl.when(g == groups - 1)
+        def _():
+            await_z(cots, czs, czr)
+            cot_y.start()
 
         for pair in range(2):
             at = pl.ds(pl.multiple_of(g * 256 + pair * 128, 128), 128)
@@ -247,20 +286,11 @@
     ]
     for copy in pool_z:
         copy.start()
-    cot_y = remote(cots.at[y_half], cots.at[y_half], cfs.at[0], cfr.at[0], y_peer)
-    cot_c = remote(cots.at[c_half], cots.at[c_half], cfs.at[1], cfr.at[1], sibling)
     pool_y = remote(pool.at[y_half], pool.at[y_half], pfs.at[0], pfr.at[0], y_peer)
     pool_c = remote(pool.at[c_half], pool.at[c_half], pfs.at[1], pfr.at[1], sibling)
 
-    def await_z(buf, sends, recvs):
-        for j in range(1, nz):
-            from_slab = slab(lax.rem(z + nz - j, nz))
-            remote(buf.at[from_slab], buf.at[from_slab], sends.at[j - 1], recvs.at[j - 1], z_peer(j)).wait_recv()
-
     await_z(pool, pzs, pzr)
     pool_y.start()
-    await_z(cots, czs, czr)
-    cot_y.start()
     remote(pool.at[y_half_in], pool.at[y_half_in], pfs.at[0], pfr.at[0], y_peer).wait_recv()
     pool_c.start()
     remote(pool.at[c_half_in], pool.at[c_half_in], pfs.at[1], pfr.at[1], sibling).wait_recv()
@@ -270,15 +300,24 @@
         remote(pp_ref, pp.at[p_got], wsend.at[0], wrecv.at[0], partner).wait_recv()
     hidden = jnp.dot(pool[...], pp[...], preferred_element_type=F32)
     sigma = 1.0 / (1.0 + jnp.exp(-hidden))
-    act[...] = (hidden * sigma).astype(BF16)
+    wide_col = lax.broadcasted_iota(jnp.int32, (n * slots, n * SLAB), 1)
+    squeeze = (wide_col >> 4) * slots + (wide_col & 15) == lax.broadcasted_iota(
+        jnp.int32, (n * slots, n * SLAB), 0
+    )
+    squeeze = jnp.where(squeeze & ((wide_col & 15) < slots), 1.0, 0.0).astype(BF16)
+    wide_row = lax.broadcasted_iota(jnp.int32, (nz * SLAB, nz * slots), 0)
+    spread = (wide_row >> 4) * slots + (wide_row & 15) == lax.broadcasted_iota(
+        jnp.int32, (nz * SLAB, nz * slots), 1
+    )
+    spread = jnp.where(spread & ((wide_row & 15) < slots), 1.0, 0.0).astype(BF16)
+    activation = (hidden * sigma).astype(BF16)
+    act[...] = jnp.dot(squeeze, activation, preferred_element_type=F32).astype(BF16)
     slope = sigma * (1.0 + hidden * (1.0 - sigma))
 
     l_local.wait()
-    if exchange:
-        remote(lp_ref, lp.at[:, l_got], wsend.at[1], wrecv.at[1], partner).wait_recv()
-
-    mine = pl.ds(pl.multiple_of(core * half, SLAB), half)
-    theirs = pl.ds(pl.multiple_of((1 - core) * half, SLAB), half)
+
+    mine = pl.ds(pl.multiple_of(core * tight, SLAB), tight)
+    theirs = pl.ds(pl.multiple_of((1 - core) * tight, SLAB), tight)
 
     def to_sibling(c):
         return remote(sib_out.at[c], sib_in.at[c], rss.at[c], rsr.at[c], sibling)
@@ -287,42 +326,46 @@
         return remote(y_out.at[c], y_in.at[c], rys.at[c], ryr.at[c], y_peer)
 
     def to_z(c, j):
-        return remote(z_out.at[c, j - 1], z_in.at[c, j - 1], rzs.at[c, j - 1], rzr.at[c, j - 1], z_peer(j))
+        there = pl.ds(pl.multiple_of(lax.rem(z + j, nz) * SLAB, SLAB), SLAB)
+        return remote(z_out.at[c, there], z_in.at[c, j - 1], rzs.at[c, j - 1], rzr.at[c, j - 1], z_peer(j))
 
     def c_cols(c):
+        if exchange:
+            c = lax.rem(c + d * (lat_chunks // 2), lat_chunks)
         return pl.ds(pl.multiple_of(c * cw, 128), cw)
 
-    @pl.loop(0, lat_chunks)
-    def _(c):
+    def product(c):
         w = lp[:, c_cols(c)]
         sib_out[c] = jnp.dot(act[theirs, :], w, preferred_element_type=F32).astype(BF16)
         to_sibling(c).start()
         own[c] = jnp.dot(act[mine, :], w, preferred_element_type=F32)
 
+    pl.loop(0, lat_chunks // 2)(product)
+    if exchange:
+        remote(lp_ref, lp.at[:, l_got], wsend.at[1], wrecv.at[1], partner).wait_recv()
+    pl.loop(lat_chunks // 2, lat_chunks)(product)
+
     remote(cots.at[y_half_in], cots.at[y_half_in], cfs.at[0], cfr.at[0], y_peer).wait_recv()
     cot_c.start()
 
     def y_step(c):
         to_sibling(c).wait_recv()
-        there = pl.ds(pl.multiple_of((1 - y) * quarter, SLAB), quarter)
-        here = pl.ds(pl.multiple_of(y * quarter, SLAB), quarter)
+        there = pl.ds(pl.multiple_of((1 - y) * (tight // 2), SLAB), tight // 2)
+        here = pl.ds(pl.multiple_of(y * (tight // 2), SLAB), tight // 2)
         y_out[c] = (own[c, there, :] + sib_in[c, there, :].astype(F32)).astype(BF16)
         to_y(c).start()
         own[c, here, :] = own[c, here, :] + sib_in[c, here, :].astype(F32)
 
     def z_step(c):
         to_y(c).wait_recv()
+        here = pl.ds(pl.multiple_of(y * (tight // 2), SLAB), tight // 2)
+        total = (own[c, here, :] + y_in[c].astype(F32)).astype(BF16)
+        z_out[c] = jnp.dot(spread, total, preferred_element_type=F32).astype(BF16)
         for j in range(1, nz):
-            zz = lax.rem(z + j, nz)
-            at = pl.ds(pl.multiple_of(y * quarter + zz * SLAB, SLAB), SLAB)
-            got = pl.ds(pl.multiple_of(zz * SLAB, SLAB), SLAB)
-            z_out[c, j - 1] = (own[c, at, :] + y_in[c, got, :].astype(F32)).astype(BF16)
             to_z(c, j).start()
 
     def last_step(c):
-        at = pl.ds(pl.multiple_of(y * quarter + z * SLAB, SLAB), SLAB)
-        got = pl.ds(pl.multiple_of(z * SLAB, SLAB), SLAB)
-        total = own[c, at, :] + y_in[c, got, :].astype(F32)
+        total = z_out[c, pl.ds(pl.multiple_of(z * SLAB, SLAB), SLAB), :].astype(F32)
         for j in range(1, nz):
             to_z(c, j).wait_recv()
             total = total + z_in[c, j - 1].astype(F32)
@@ -332,7 +375,7 @@
 
     remote(cots.at[c_half_in], cots.at[c_half_in], cfs.at[1], cfr.at[1], sibling).wait_recv()
     back = lax.dot_general(cots[...], lp[...], NT, preferred_element_type=F32)
-    act[...] = (back * slope).astype(BF16)
+    act[...] = jnp.dot(squeeze, (back * slope).astype(BF16), preferred_element_type=F32).astype(BF16)
     g = lat_chunks
     sib_out[g] = lax.dot_general(act[theirs, :], pp[...], NT, preferred_element_type=F32).astype(BF16)
     to_sibling(g).start()
@@ -396,7 +439,7 @@
     cw = width
     chunks = wide // cw + 1
     groups = width // 256
-    half = n // 2 * SLAB
+    half = n // 2 * slots
     vmem = pl.BlockSpec(memory_space=pltpu.VMEM)
     hbm = pl.BlockSpec(memory_space=pl.ANY)
     dma = pltpu.SemaphoreType.DMA
@@ -406,9 +449,14 @@
             jax.ShapeDtypeStruct((slots, wide), BF16),
             jax.ShapeDtypeStruct((slots, width), BF16),
         ),
-        in_specs=[pl.BlockSpec(memory_space=pltpu.SMEM), vmem, vmem, vmem, vmem, hbm, hbm],
+        in_specs=[hbm] * 7,
         out_specs=(vmem, vmem),
         scratch_shapes=[
+            pltpu.SMEM((1, slots), jnp.int32),
+            pltpu.VMEM((rows, width), BF16),
+            pltpu.VMEM((rows, width), BF16),
+            pltpu.VMEM((rows, width), BF16),
+            pltpu.VMEM((slots, wide), BF16),
             pltpu.VMEM((2, rows, width), BF16),
             pltpu.VMEM((2, rows, width), BF16),
             pltpu.VMEM((rows, width), BF16),
@@ -416,14 +464,15 @@
             pltpu.VMEM((n * SLAB, wide), BF16),
             pltpu.VMEM((width, block), BF16),
             pltpu.VMEM((block, wide), BF16),
-            pltpu.VMEM((n * SLAB, block), BF16),
+            pltpu.VMEM((n * slots, block), BF16),
             pltpu.VMEM((chunks, half, cw), F32),
             pltpu.VMEM((chunks, half, cw), BF16),
             pltpu.VMEM((chunks, half, cw), BF16),
             pltpu.VMEM((chunks, half // 2, cw), BF16),
             pltpu.VMEM((chunks, half // 2, cw), BF16),
+            pltpu.VMEM((chunks, nz * SLAB, cw), BF16),
             pltpu.VMEM((chunks, nz - 1, SLAB, cw), BF16),
-            pltpu.VMEM((chunks, nz - 1, SLAB, cw), BF16),
+            dma((5,)),
             dma((2,)),
             dma((2,)),
             dma((2,)),
@@ -447,7 +496,7 @@
             dma((chunks, nz - 1)),
         ],
         compiler_params=pltpu.CompilerParams(
-            collective_id=0, has_side_effects=True, vmem_limit_bytes=44 * 2**20
+            collective_id=0, has_side_effects=True, vmem_limit_bytes=60 * 2**20
         ),
         cost_estimate=pl.CostEstimate(flops=2 * 10**9, bytes_accessed=4 * 10**6, transcendentals=10**6),
     )(

time: 79.1 us -> 73.8 us (0.933)
  local copies, waits for them, and re-layouts: 7.85 us -> 2.19 us
    unnamed x16 -> x4, local copies, waits for them, and re-layouts: 7.85 us -> 2.19 us
where the time goes in v2:
time: 73.8 us; the launch traced here: 73.7 us
  Pallas kernels  70.8 us (96%)
  local copies, waits for them, and re-layouts  2.19 us (3%)
    pallas_call x1, Pallas kernels, per_device(): pl.pallas_call(functools.partial(kernel, n, exchange), out_shape=(jax.Sha...  70.8 us
    unnamed x4, local copies, waits for them, and re-layouts  2.19 us

profile of v2, /device:TPU:0, one launch (start us, length us, event | category | flops | bytes accessed | tf_op | source)
XLA Modules:
  0.0 73.7 jit_solution(3412280060741692249)
XLA Ops:
  0.6 70.8 %shard_map.86 = (bf16[12,4096]{1,0:T(8,128)(2,1)}, bf16[12,1024]{1,0:T(8,128)(2,1)}) custom-call(s32[1,12]{1,0:T(1,128)} %bitcast.13, bf16[128,1024]{1,0:T(8,128)(2,1)} %bitcast.9, bf16[128,1024]{1,0:T(8,128)(2,1)} %bitcast.10, bf16[128,1024]{1,0:T(8,128)(2,1)} %bitcast.11, bf16[12,4096]{1,0:T(8,128)(2,1)} %bitcast.12, bf16[512,256]{1,0:T(8,128)(2,1)} %pp_ref.1, ...), custom_call_target="tpu_custom_call" | custom-call | flops 2000000000 | bytes 4000000 | tf_op jit(solution)/shard_map/pallas_call | solution.py:446
  71.5 0.0 copy-start
  71.5 1.6 %copy.11 = bf16[1,12,4096]{2,1,0:T(8,128)(2,1)} copy(bf16[1,12,4096]{2,1,0:T(8,128)(2,1)} %bitcast.7) | data formatting | bytes 196608
  73.1 0.0 copy-done
  73.1 0.6 copy.12
Async XLA Ops:
  71.5 1.6 %copy-start = (bf16[12,1024]{1,0:T(8,128)(2,1)S(1)}, bf16[12,1024]{1,0:T(8,128)(2,1)}, u32[]{:S(2)}) copy-start(bf16[12,1024]{1,0:T(8,128)(2,1)} %get-tuple-element.5) | copy-start | bytes 73732

commit v3 on v2

--- a/solution.py
+++ b/solution.py
@@ -310,6 +310,18 @@
         jnp.int32, (nz * SLAB, nz * slots), 1
     )
     spread = jnp.where(spread & ((wide_row & 15) < slots), 1.0, 0.0).astype(BF16)
+    extra = SLAB - slots
+    packs = slots // extra
+    part = cw // (packs + 1)
+    tight_col = lax.broadcasted_iota(jnp.int32, (nz * SLAB, nz * slots), 1)
+    small_row = lax.broadcasted_iota(jnp.int32, (SLAB, SLAB), 0)
+    small_col = lax.broadcasted_iota(jnp.int32, (SLAB, SLAB), 1)
+    folds, unfolds = [], []
+    for k in range(packs):
+        fold = (wide_row >> 4) * slots + (wide_row & 15) - slots + extra * k == tight_col
+        folds.append(jnp.where(fold & ((wide_row & 15) >= slots), 1.0, 0.0).astype(BF16))
+        unfold = (small_col == small_row + slots - extra * k) & (small_col >= slots)
+        unfolds.append(jnp.where(unfold, 1.0, 0.0).astype(BF16))
     activation = (hidden * sigma).astype(BF16)
     act[...] = jnp.dot(squeeze, activation, preferred_element_type=F32).astype(BF16)
     slope = sigma * (1.0 + hidden * (1.0 - sigma))
@@ -360,7 +372,12 @@
         to_y(c).wait_recv()
         here = pl.ds(pl.multiple_of(y * (tight // 2), SLAB), tight // 2)
         total = (own[c, here, :] + y_in[c].astype(F32)).astype(BF16)
-        z_out[c] = jnp.dot(spread, total, preferred_element_type=F32).astype(BF16)
+        tail = total[:, packs * part :]
+        for k in range(packs):
+            at = slice(k * part, (k + 1) * part)
+            piece = jnp.dot(spread, total[:, at], preferred_element_type=F32)
+            piece += jnp.dot(folds[k], tail, preferred_element_type=F32)
+            z_out[c, :, at] = piece.astype(BF16)
         for j in range(1, nz):
             to_z(c, j).start()
 
@@ -369,20 +386,28 @@
         for j in range(1, nz):
             to_z(c, j).wait_recv()
             total = total + z_in[c, j - 1].astype(F32)
-        return total
+        total = total.astype(BF16)
+        tail = jnp.zeros((SLAB, part), F32)
+        for k in range(packs):
+            tail += jnp.dot(unfolds[k], total[:, k * part : (k + 1) * part], preferred_element_type=F32)
+        return jnp.concatenate([total.astype(F32), tail], axis=1)
 
     pl.loop(0, lat_chunks)(y_step)
 
     remote(cots.at[c_half_in], cots.at[c_half_in], cfs.at[1], cfr.at[1], sibling).wait_recv()
-    back = lax.dot_general(cots[...], lp[...], NT, preferred_element_type=F32)
+    z_step(0)
+    mid = lp.shape[1] // 2
+    back = lax.dot_general(cots[:, :mid], lp[:, :mid], NT, preferred_element_type=F32)
+    z_step(1)
+    back += lax.dot_general(cots[:, mid:], lp[:, mid:], NT, preferred_element_type=F32)
     act[...] = jnp.dot(squeeze, (back * slope).astype(BF16), preferred_element_type=F32).astype(BF16)
     g = lat_chunks
     sib_out[g] = lax.dot_general(act[theirs, :], pp[...], NT, preferred_element_type=F32).astype(BF16)
     to_sibling(g).start()
     own[g] = lax.dot_general(act[mine, :], pp[...], NT, preferred_element_type=F32)
+    z_step(2)
     y_step(g)
-
-    pl.loop(0, chunks)(z_step)
+    pl.loop(3, chunks)(z_step)
 
     @pl.loop(0, lat_chunks)
     def _(c):
@@ -470,8 +495,8 @@
             pltpu.VMEM((chunks, half, cw), BF16),
             pltpu.VMEM((chunks, half // 2, cw), BF16),
             pltpu.VMEM((chunks, half // 2, cw), BF16),
-            pltpu.VMEM((chunks, nz * SLAB, cw), BF16),
-            pltpu.VMEM((chunks, nz - 1, SLAB, cw), BF16),
+            pltpu.VMEM((chunks, nz * SLAB, cw * slots // SLAB), BF16),
+            pltpu.VMEM((chunks, nz - 1, SLAB, cw * slots // SLAB), BF16),
             dma((5,)),
             dma((2,)),
             dma((2,)),

time: 73.8 us -> 74.8 us (1.014)
  Pallas kernels: 70.8 us -> 71.8 us
    pallas_call x1, Pallas kernels: 70.8 us -> 71.8 us  [per_device(): pl.pallas_call(functools.partial(kernel, n, exchange), out_shape=(jax.Sha...]
where the time goes in v3:
time: 74.8 us; the launch traced here: 74.6 us
  Pallas kernels  71.8 us (96%)
  local copies, waits for them, and re-layouts  2.19 us (3%)
    pallas_call x1, Pallas kernels, per_device(): pl.pallas_call(functools.partial(kernel, n, exchange), out_shape=(jax.Sha...  71.8 us
    unnamed x4, local copies, waits for them, and re-layouts  2.19 us

profile of v3, /device:TPU:0, one launch (start us, length us, event | category | flops | bytes accessed | tf_op | source)
XLA Modules:
  0.0 74.6 jit_solution(11695400790049752210)
XLA Ops:
  0.6 71.8 %shard_map.86 = (bf16[12,4096]{1,0:T(8,128)(2,1)}, bf16[12,1024]{1,0:T(8,128)(2,1)}) custom-call(s32[1,12]{1,0:T(1,128)} %bitcast.13, bf16[128,1024]{1,0:T(8,128)(2,1)} %bitcast.9, bf16[128,1024]{1,0:T(8,128)(2,1)} %bitcast.10, bf16[128,1024]{1,0:T(8,128)(2,1)} %bitcast.11, bf16[12,4096]{1,0:T(8,128)(2,1)} %bitcast.12, bf16[512,256]{1,0:T(8,128)(2,1)} %pp_ref.1, ...), custom_call_target="tpu_custom_call" | custom-call | flops 2000000000 | bytes 4000000 | tf_op jit(solution)/shard_map/pallas_call | solution.py:471
  72.4 0.0 copy-start
  72.5 1.6 %copy.11 = bf16[1,12,4096]{2,1,0:T(8,128)(2,1)} copy(bf16[1,12,4096]{2,1,0:T(8,128)(2,1)} %bitcast.7) | data formatting | bytes 196608
  74.0 0.0 copy-done
  74.0 0.6 copy.12
Async XLA Ops:
  72.4 1.6 %copy-start = (bf16[12,1024]{1,0:T(8,128)(2,1)S(1)}, bf16[12,1024]{1,0:T(8,128)(2,1)}, u32[]{:S(2)}) copy-start(bf16[12,1024]{1,0:T(8,128)(2,1)} %get-tuple-element.5) | copy-start | bytes 73732

commit v4 on v3

--- a/solution.py
+++ b/solution.py
@@ -187,8 +187,6 @@
         remote(cots.at[my_slab], cots.at[my_slab], czs.at[j - 1], czr.at[j - 1], z_peer(j))
         for j in range(1, nz)
     ]
-    for copy in cot_z:
-        copy.start()
     p_local.start()
     l_local.start()
 
@@ -255,8 +253,8 @@
 
         @pl.when(g == groups - 1)
         def _():
-            await_z(cots, czs, czr)
-            cot_y.start()
+            for copy in cot_z:
+                copy.start()
 
         for pair in range(2):
             at = pl.ds(pl.multiple_of(g * 256 + pair * 128, 128), 128)
@@ -293,6 +291,8 @@
     pool_y.start()
     remote(pool.at[y_half_in], pool.at[y_half_in], pfs.at[0], pfr.at[0], y_peer).wait_recv()
     pool_c.start()
+    await_z(cots, czs, czr)
+    cot_y.start()
     remote(pool.at[c_half_in], pool.at[c_half_in], pfs.at[1], pfr.at[1], sibling).wait_recv()
 
     p_local.wait()
@@ -357,9 +357,6 @@
         remote(lp_ref, lp.at[:, l_got], wsend.at[1], wrecv.at[1], partner).wait_recv()
     pl.loop(lat_chunks // 2, lat_chunks)(product)
 
-    remote(cots.at[y_half_in], cots.at[y_half_in], cfs.at[0], cfr.at[0], y_peer).wait_recv()
-    cot_c.start()
-
     def y_step(c):
         to_sibling(c).wait_recv()
         there = pl.ds(pl.multiple_of((1 - y) * (tight // 2), SLAB), tight // 2)
@@ -394,20 +391,19 @@
 
     pl.loop(0, lat_chunks)(y_step)
 
+    pl.loop(0, 2)(z_step)
+    remote(cots.at[y_half_in], cots.at[y_half_in], cfs.at[0], cfr.at[0], y_peer).wait_recv()
+    cot_c.start()
+    pl.loop(2, lat_chunks)(z_step)
     remote(cots.at[c_half_in], cots.at[c_half_in], cfs.at[1], cfr.at[1], sibling).wait_recv()
-    z_step(0)
-    mid = lp.shape[1] // 2
-    back = lax.dot_general(cots[:, :mid], lp[:, :mid], NT, preferred_element_type=F32)
-    z_step(1)
-    back += lax.dot_general(cots[:, mid:], lp[:, mid:], NT, preferred_element_type=F32)
+    back = lax.dot_general(cots[...], lp[...], NT, preferred_element_type=F32)
     act[...] = jnp.dot(squeeze, (back * slope).astype(BF16), preferred_element_type=F32).astype(BF16)
     g = lat_chunks
     sib_out[g] = lax.dot_general(act[theirs, :], pp[...], NT, preferred_element_type=F32).astype(BF16)
     to_sibling(g).start()
     own[g] = lax.dot_general(act[mine, :], pp[...], NT, preferred_element_type=F32)
-    z_step(2)
     y_step(g)
-    pl.loop(3, chunks)(z_step)
+    z_step(g)
 
     @pl.loop(0, lat_chunks)
     def _(c):

time: 74.8 us -> 72.3 us (0.967)
  Pallas kernels: 71.8 us -> 69.3 us
    pallas_call x1, Pallas kernels: 71.8 us -> 69.3 us  [per_device(): pl.pallas_call(functools.partial(kernel, n, exchange), out_shape=(jax.Sha...]
where the time goes in v4:
time: 72.3 us; the launch traced here: 72.1 us
  Pallas kernels  69.3 us (96%)
  local copies, waits for them, and re-layouts  2.19 us (3%)
    pallas_call x1, Pallas kernels, per_device(): pl.pallas_call(functools.partial(kernel, n, exchange), out_shape=(jax.Sha...  69.3 us
    unnamed x4, local copies, waits for them, and re-layouts  2.19 us

profile of v4, /device:TPU:0, one launch (start us, length us, event | category | flops | bytes accessed | tf_op | source)
XLA Modules:
  0.0 72.1 jit_solution(18120426118428117950)
XLA Ops:
  0.6 69.3 %shard_map.86 = (bf16[12,4096]{1,0:T(8,128)(2,1)}, bf16[12,1024]{1,0:T(8,128)(2,1)}) custom-call(s32[1,12]{1,0:T(1,128)} %bitcast.13, bf16[128,1024]{1,0:T(8,128)(2,1)} %bitcast.9, bf16[128,1024]{1,0:T(8,128)(2,1)} %bitcast.10, bf16[128,1024]{1,0:T(8,128)(2,1)} %bitcast.11, bf16[12,4096]{1,0:T(8,128)(2,1)} %bitcast.12, bf16[512,256]{1,0:T(8,128)(2,1)} %pp_ref.1, ...), custom_call_target="tpu_custom_call" | custom-call | flops 2000000000 | bytes 4000000 | tf_op jit(solution)/shard_map/pallas_call | solution.py:467
  69.9 0.0 copy-start
  69.9 1.6 %copy.11 = bf16[1,12,4096]{2,1,0:T(8,128)(2,1)} copy(bf16[1,12,4096]{2,1,0:T(8,128)(2,1)} %bitcast.7) | data formatting | bytes 196608
  71.5 0.0 copy-done
  71.5 0.6 copy.12
Async XLA Ops:
  69.9 1.6 %copy-start = (bf16[12,1024]{1,0:T(8,128)(2,1)S(1)}, bf16[12,1024]{1,0:T(8,128)(2,1)}, u32[]{:S(2)}) copy-start(bf16[12,1024]{1,0:T(8,128)(2,1)} %get-tuple-element.5) | copy-start | bytes 73732

commit v5 on v4

--- a/solution.py
+++ b/solution.py
@@ -291,8 +291,6 @@
     pool_y.start()
     remote(pool.at[y_half_in], pool.at[y_half_in], pfs.at[0], pfr.at[0], y_peer).wait_recv()
     pool_c.start()
-    await_z(cots, czs, czr)
-    cot_y.start()
     remote(pool.at[c_half_in], pool.at[c_half_in], pfs.at[1], pfr.at[1], sibling).wait_recv()
 
     p_local.wait()
@@ -353,6 +351,8 @@
         own[c] = jnp.dot(act[mine, :], w, preferred_element_type=F32)
 
     pl.loop(0, lat_chunks // 2)(product)
+    await_z(cots, czs, czr)
+    cot_y.start()
     if exchange:
         remote(lp_ref, lp.at[:, l_got], wsend.at[1], wrecv.at[1], partner).wait_recv()
     pl.loop(lat_chunks // 2, lat_chunks)(product)

time: 72.3 us -> 75.8 us (1.048)
  Pallas kernels: 69.3 us -> 72.8 us
    pallas_call x1, Pallas kernels: 69.3 us -> 72.8 us  [per_device(): pl.pallas_call(functools.partial(kernel, n, exchange), out_shape=(jax.Sha...]
where the time goes in v5:
time: 75.8 us; the launch traced here: 75.6 us
  Pallas kernels  72.8 us (96%)
  local copies, waits for them, and re-layouts  2.19 us (3%)
    pallas_call x1, Pallas kernels, per_device(): pl.pallas_call(functools.partial(kernel, n, exchange), out_shape=(jax.Sha...  72.8 us
    unnamed x4, local copies, waits for them, and re-layouts  2.19 us

profile of v5, /device:TPU:0, one launch (start us, length us, event | category | flops | bytes accessed | tf_op | source)
XLA Modules:
  0.0 75.6 jit_solution(13923558485469726184)
XLA Ops:
  0.6 72.8 %shard_map.86 = (bf16[12,4096]{1,0:T(8,128)(2,1)}, bf16[12,1024]{1,0:T(8,128)(2,1)}) custom-call(s32[1,12]{1,0:T(1,128)} %bitcast.13, bf16[128,1024]{1,0:T(8,128)(2,1)} %bitcast.9, bf16[128,1024]{1,0:T(8,128)(2,1)} %bitcast.10, bf16[128,1024]{1,0:T(8,128)(2,1)} %bitcast.11, bf16[12,4096]{1,0:T(8,128)(2,1)} %bitcast.12, bf16[512,256]{1,0:T(8,128)(2,1)} %pp_ref.1, ...), custom_call_target="tpu_custom_call" | custom-call | flops 2000000000 | bytes 4000000 | tf_op jit(solution)/shard_map/pallas_call | solution.py:467
  73.4 0.0 copy-start
  73.4 1.6 %copy.11 = bf16[1,12,4096]{2,1,0:T(8,128)(2,1)} copy(bf16[1,12,4096]{2,1,0:T(8,128)(2,1)} %bitcast.7) | data formatting | bytes 196608
  75.0 0.0 copy-done
  75.0 0.6 copy.12
Async XLA Ops:
  73.4 1.6 %copy-start = (bf16[12,1024]{1,0:T(8,128)(2,1)S(1)}, bf16[12,1024]{1,0:T(8,128)(2,1)}, u32[]{:S(2)}) copy-start(bf16[12,1024]{1,0:T(8,128)(2,1)} %get-tuple-element.5) | copy-start | bytes 73732
